TPU v7x, 512 devices: a whole 4x4x16 slice. The times are simulated.
512 devices in a mesh: seq: 128 (over x, z, core), head: 4 (over y).
Axes of the slice: x: 4, y: 4, z: 16, core: 2. Of those that a mesh axis runs over, the one named last changes fastest.
Arguments:
- tile_rows: bfloat16 [65536, 512], P('seq', 'head'), as said below
- tile_order: int32 [65536], P('seq'), may hold values from 0 to 65535, as said below
- tissue_mask: int32 [65536], P('seq'), may hold values from 0 to 1, as said below
- conv_weight: bfloat16 [512, 64, 512], P('seq', None, 'head'), may hold values from -0.03125 to 0.03125
- conv_bias: float32 [512], P('head'), may hold values from -3 to 3
- norm_gain: float32 [512], P('head'), may hold values from 0.1 to 1.9
- norm_bias: float32 [512], P('head'), may hold values from -3 to 3
- query_weight: bfloat16 [512, 512], P(None, 'head'), may hold values from -0.796875 to 0.796875
- key_weight: bfloat16 [512, 512], P(None, 'head'), may hold values from -0.25 to 0.25
- value_weight: bfloat16 [512, 512], P(None, 'head'), may hold values from -0.25 to 0.25
- out_weight: bfloat16 [512, 512], P('head'), may hold values from -0.25 to 0.25
Outputs:
- attention_out: bfloat16 [65536, 512], P('seq', 'head')
Inputs may be any that keep to these rules, and one draw needn't show every extreme that they name: `tile_rows`: features of the tiles. `tile_order`: A permutation of the grid positions. Grid blocks of 8 x 8 tiles are numbered row-major and owned in runs of 8 by the indices of seq in order; of the 512 tiles of one index of seq, at most 8 lie in the blocks of one owner, and every index of seq has 8 in the blocks of some owner. `tissue_mask`: 1 marks tissue, 0 background.
All inputs are finite; a program needn't handle non-finite values.
Results may differ from a plain program's by a relative error of at most 0.015.
The roundings to bfloat16 on the way count: a program that leaves them out, or rounds other values in their place, can miss the bound.
Values may be sent and summed in bfloat16 or wider, within the bound.
No kernel may reach another device: no remote copies, remote signals or barrier semaphores. Data moves between devices by JAX's collectives and lax.ppermute only.
A program may use at most 64 MiB of HBM per device.

v0:
```python
import math
import jax
import jax.numpy as jnp
from jax import lax
from jax.sharding import PartitionSpec as P

HEAD_SIZE = 64
REDUCE = 8
GRID_W = 512


def block_step(count):
    best = 1
    for candidate in range(1, min(count, 512) + 1):
        if count % candidate == 0:
            best = candidate
    return best


def make_fold(queries, heads_here, scale):

    def fold(carry, piece, start):
        count = piece.shape[0]
        step = block_step(count)
        blocks = piece.reshape(count // step, step, piece.shape[1])
        split_at = heads_here * HEAD_SIZE

        def visit(state, key_block):
            highest, totals, accum = state
            keys3 = key_block[:, :split_at].reshape(step, heads_here, HEAD_SIZE)
            values3 = key_block[:, split_at:].reshape(step, heads_here, HEAD_SIZE)
            scores = (
                jnp.einsum("thd,khd->htk", queries, keys3, preferred_element_type=jnp.float32)
                * scale
            )
            newest = jnp.maximum(highest, jnp.max(scores, -1))
            shrink = jnp.exp(highest - newest)
            weights = jnp.exp(scores - newest[:, :, None])
            totals = totals * shrink + jnp.sum(weights, -1)
            update = jnp.einsum(
                "htk,khd->thd",
                weights.astype(jnp.bfloat16),
                values3,
                preferred_element_type=jnp.float32,
            )
            accum = accum * shrink.T[:, :, None] + update
            return ((newest, totals, accum), None)

        carry, unused = lax.scan(visit, carry, blocks)
        return carry

    return fold


def local(
    tile_rows,
    tile_order,
    tissue_mask,
    conv_weight,
    conv_bias,
    norm_gain,
    norm_bias,
    query_weight,
    key_weight,
    value_weight,
    out_weight,
):
    devices = lax.axis_size("seq")
    local_rows, quarter = tile_rows.shape
    width = query_weight.shape[0]
    patch = conv_weight.shape[1]
    blocks_here = local_rows // patch
    capacity = 2 * (local_rows // devices)
    flags = tissue_mask.astype(jnp.bfloat16)
    masked = tile_rows * flags[:, None]
    grid_row = tile_order // GRID_W
    grid_col = tile_order % GRID_W
    block = grid_row // REDUCE * (GRID_W // REDUCE) + grid_col // REDUCE
    offset = grid_row % REDUCE * REDUCE + grid_col % REDUCE
    owner = block // blocks_here
    target = block % blocks_here * patch + offset
    onehot = (owner[:, None] == jnp.arange(devices, dtype=jnp.int32)[None, :]).astype(jnp.int32)
    ranks = jnp.sum(onehot * (jnp.cumsum(onehot, 0) - 1), 1)
    outgoing = jnp.zeros((devices, capacity, quarter), jnp.bfloat16).at[owner, ranks].set(masked)
    where_to = jnp.full((devices, capacity), -1, jnp.int32).at[owner, ranks].set(target)
    incoming, arrived = (
        lax.all_to_all(outgoing, "seq", split_axis=0, concat_axis=0, tiled=True),
        lax.all_to_all(where_to, "seq", split_axis=0, concat_axis=0, tiled=True),
    )
    places = arrived.reshape(-1)
    places = jnp.where(places >= 0, places, local_rows)
    patches = (
        jnp.zeros((local_rows + 1, quarter), jnp.bfloat16)
        .at[places]
        .set(incoming.reshape(-1, quarter))
    )
    patches = patches[:local_rows].reshape(blocks_here, patch, quarter)
    partial_conv = jnp.einsum(
        "bpc,opc->bo",
        patches,
        lax.all_gather(conv_weight, "seq", axis=0, tiled=True),
        preferred_element_type=jnp.float32,
    )
    shares = (
        lax.psum_scatter(partial_conv, "head", scatter_dimension=1, tiled=True) + conv_bias[None, :]
    )
    first_sum, second_sum = lax.psum((jnp.sum(shares, 1), jnp.sum(shares * shares, 1)), "head")
    center = (first_sum / width)[:, None]
    spread = (second_sum / width)[:, None]
    normed_share = (
        (shares - center) * lax.rsqrt(spread - center * center + 1e-05) * norm_gain + norm_bias
    ).astype(jnp.bfloat16)
    normed = lax.all_gather(normed_share, "head", axis=1, tiled=True)
    keys_here = jnp.dot(normed, key_weight, preferred_element_type=jnp.float32).astype(jnp.bfloat16)
    values_here = jnp.dot(normed, value_weight, preferred_element_type=jnp.float32).astype(
        jnp.bfloat16
    )
    key_value = jnp.concatenate([keys_here, values_here], 1)
    features = lax.all_gather(tile_rows, "head", axis=1, tiled=True)
    heads_here = quarter // HEAD_SIZE
    queries = jnp.dot(features, query_weight, preferred_element_type=jnp.float32).astype(
        jnp.bfloat16
    )
    queries = queries.reshape(local_rows, heads_here, HEAD_SIZE)
    scale = 1.0 / math.sqrt(HEAD_SIZE)
    start_state = (
        jnp.full((heads_here, local_rows), -1e30, jnp.float32),
        jnp.zeros((heads_here, local_rows), jnp.float32),
        jnp.zeros((local_rows, heads_here, HEAD_SIZE), jnp.float32),
    )
    folder = make_fold(queries, heads_here, scale)
    every_key = lax.all_gather(key_value, "seq", axis=0, tiled=True)
    highest, totals, accum = folder(start_state, every_key, 0)
    attended = (accum / totals.T[:, :, None]).reshape(local_rows, quarter).astype(jnp.bfloat16)
    projected = jnp.dot(attended, out_weight, preferred_element_type=jnp.float32)
    summed = lax.psum_scatter(
        projected.astype(jnp.bfloat16), "head", scatter_dimension=1, tiled=True
    ).astype(jnp.float32)
    return (summed * tissue_mask[:, None].astype(jnp.float32)).astype(jnp.bfloat16)


def solution(mesh):
    return jax.shard_map(
        local,
        mesh=mesh,
        in_specs=(
            P("seq", "head"),
            P("seq"),
            P("seq"),
            P("seq", None, "head"),
            P("head"),
            P("head"),
            P("head"),
            P(None, "head"),
            P(None, "head"),
            P(None, "head"),
            P("head", None),
        ),
        out_specs=P("seq", "head"),
        check_vma=False,
    )
```

profile of v0, /device:TPU:2, one launch (start us, length us, event | category | flops | bytes accessed | tf_op | source)
XLA Modules:
  0.0 349.9 jit_solution(16431818356530717991)
XLA Ops:
  6.5 0.7 all-gather.2.cloned.1.call-update
  7.3 0.7 fusion.28
  8.7 22.0 %scatter_fusion = s32[128,8]{0,1:T(8,128)S(1)} fusion(s32[128,8]{0,1:T(8,128)S(1)} %broadcast_in_dim.22, s32[512]{0:T(512)S(1)} %bitcast.79, s32[512]{0:T(512)S(1)} %get-tuple-element.97), kind=kCustom, calls=%fused_computation | custom fusion | bytes 10240 | tf_op jit(solution)/shard_map/scatter | solution.py:85
  30.7 0.7 copy.25
  31.5 19.5 %all-to-all-start = ((s32[128,1,8]{2,1,0:T(1,128)}), s32[128,1,8]{2,1,0:T(1,128)S(1)}, u32[]{:S(2)}, u32[]{:S(2)}) async-start(s32[128,1,8]{2,1,0:T(1,128)} %copy.25), calls=%async_computation | async-start | bytes 131072 | tf_op jit(solution)/shard_map/all_to_all | solution.py:88
  51.2 0.7 broadcast_in_dim.48
  51.9 51.3 %scatter_fusion.1 = bf16[128,8,128]{2,1,0:T(8,128)(2,1)} fusion(bf16[128,8,128]{2,1,0:T(8,128)(2,1)} %broadcast_in_dim.48, s32[512]{0:T(512)S(1)} %bitcast.80, bf16[512,128]{1,0:T(8,128)(2,1)S(1)} %broadcast_multiply_fusion), kind=kCustom, calls=%fused_computation.1 | custom fusion | bytes 397312 | tf_op jit(solution)/shard_map/scatter | solution.py:84
  103.3 16.2 %all-to-all-start.1 = ((bf16[128,8,128]{2,1,0:T(8,128)(2,1)}), bf16[128,8,128]{2,1,0:T(8,128)(2,1)S(1)}, u32[]{:S(2)}, u32[]{:S(2)}) async-start(bf16[128,8,128]{2,1,0:T(8,128)(2,1)} %scatter_fusion.1), calls=%async_computation.1 | async-start | bytes 524288 | tf_op jit(solution)/shard_map/all_to_all | solution.py:87
  119.5 14.0 %all_gather.15 = bf16[512,512]{1,0:T(8,128)(2,1)S(1)} all-gather(bf16[512,128]{1,0:T(8,128)(2,1)S(1)} %copy-done.1), channel_id=1, replica_groups=mesh['seq'=128,'head'=4] {'head'}, dimensions={1}, use_global_device_ids=true | all-gather | bytes 655360 | tf_op jit(solution)/shard_map/all_gather | solution.py:119
  133.5 0.5 broadcast.298
  134.0 0.8 reduce.3
  135.0 9.7 %all-to-all-done.1 = bf16[128,8,128]{2,1,0:T(8,128)(2,1)S(1)} async-done(((bf16[128,8,128]{2,1,0:T(8,128)(2,1)}), bf16[128,8,128]{2,1,0:T(8,128)(2,1)S(1)}, u32[]{:S(2)}, u32[]{:S(2)}) %all-to-all-start.1) | async-done | bytes 262176 | tf_op jit(solution)/shard_map/all_to_all | solution.py:87
  144.7 3.4 scatter_custom_fusion.2
  148.1 20.0 %all-gather.2.cloned.1.call-done = bf16[512,64,128]{2,1,0:T(8,128)(2,1)} async-done(((bf16[4,64,128]{2,1,0:T(8,128)(2,1)}), bf16[512,64,128]{2,1,0:T(8,128)(2,1)}) %all-gather.2.cloned.1.call-update) | async-done | bytes 8388624 | tf_op jit(solution)/shard_map/all_gather | solution.py:101
  168.1 12.4 %fusion.13 = f32[8,512]{1,0:T(8,128)} fusion(bf16[512,64,128]{2,1,0:T(8,128)(2,1)} %all-gather.2.cloned.1.call-done, bf16[8,64,128]{2,1,0:T(8,128)(2,1)S(1)} %bitcast.87), kind=kOutput, calls=%fused_computation.25 | convolution fusion | flops 67108864 | bytes 8536064 | tf_op jit(solution)/shard_map/bpc,opc->bo/dot_general | solution.py:98
  181.0 24.1 %reduce-scatter.5.cloned.1.call-done = f32[8,128]{1,0:T(8,128)} async-done(((f32[8,512]{1,0:T(8,128)}), f32[8,128]{1,0:T(8,128)}) %reduce-scatter.5.cloned.1.call-update) | async-done | bytes 4112 | tf_op jit(solution)/shard_map/reduce_scatter | solution.py:105
  205.0 0.8 add_reduce_fusion
  205.9 8.6 %all-reduce = (f32[8]{0:T(128)S(1)}, f32[8]{0:T(128)S(1)}) all-reduce(f32[8]{0:T(128)S(1)} %get-tuple-element.80, f32[8]{0:T(128)S(1)} %get-tuple-element.79), channel_id=1, replica_groups=mesh['seq'=128,'head'=4] {'head'}, use_global_device_ids=true, to_apply=%region_10.11 | all-reduce | flops 16 | bytes 128 | tf_op jit(solution)/shard_map/psum | solution.py:107
  214.4 0.8 add_convert_fusion
  215.2 10.4 %all_gather.13 = bf16[8,512]{1,0:T(8,128)(2,1)S(1)} all-gather(bf16[8,128]{1,0:T(8,128)(2,1)S(1)} %add_convert_fusion), channel_id=1, replica_groups=mesh['seq'=128,'head'=4] {'head'}, dimensions={1}, use_global_device_ids=true | all-gather | bytes 10240 | tf_op jit(solution)/shard_map/all_gather | solution.py:113
  225.8 84.1 %all_gather.14 = bf16[1024,256]{1,0:T(8,128)(2,1)S(1)} all-gather(bf16[8,256]{1,0:T(8,128)(2,1)S(1)} %pad_maximum_fusion), channel_id=1, replica_groups=mesh['seq'=128,'head'=4] {'seq'}, dimensions={0}, use_global_device_ids=true | all-gather | bytes 528384 | tf_op jit(solution)/shard_map/all_gather | solution.py:132
  309.9 3.3 while.15
  310.1 0.5 bitcast_reduce_fusion.2
  310.6 0.5 fusion.67
  311.2 0.4 fusion.65
  311.8 0.5 bitcast_reduce_fusion.2
  312.3 0.5 fusion.67
  312.8 0.4 fusion.65
  313.6 1.0 copy.30
  314.6 26.9 %reduce-scatter.7.cloned.1.call-done = bf16[128,512]{1,0:T(8,128)(2,1)} async-done(((bf16[512,512]{1,0:T(8,128)(2,1)}), bf16[128,512]{1,0:T(8,128)(2,1)}) %reduce-scatter.7.cloned.1.call-update) | async-done | bytes 131088
  341.6 1.0 copy.31
  342.6 0.8 multiply_convert_fusion
  (62 shorter events, 2.5 us)
Async XLA Ops:
  6.5 306.7 %copy-start = (bf16[128,512]{1,0:T(8,128)(2,1)S(1)}, bf16[128,512]{1,0:T(8,128)(2,1)}, u32[]{:S(2)}) copy-start(bf16[128,512]{1,0:T(8,128)(2,1)} %param.23) | copy-start | bytes 393220
  6.5 161.6 %all-gather.2.cloned.1.call-start = ((), (), s32[]{:S(2)}) async-start(), calls=%async_computation.4 | async-start | bytes 8454144 | tf_op jit(solution)/shard_map/all_gather | solution.py:101
  8.7 42.3 %copy-start.5 = (s32[512]{0:T(512)S(1)}, s32[512]{0:T(512)}, u32[]{:S(2)}) copy-start(s32[512]{0:T(512)} %param.15) | copy-start | bytes 6148
  8.7 42.3 %copy-start.1 = (bf16[512,128]{1,0:T(8,128)(2,1)S(1)}, bf16[512,128]{1,0:T(8,128)(2,1)}, u32[]{:S(2)}) copy-start(bf16[512,128]{1,0:T(8,128)(2,1)} %param.13) | copy-start | bytes 393220
  31.5 71.8 %all-to-all-start = ((s32[128,1,8]{2,1,0:T(1,128)}), s32[128,1,8]{2,1,0:T(1,128)S(1)}, u32[]{:S(2)}, u32[]{:S(2)}) async-start(s32[128,1,8]{2,1,0:T(1,128)} %copy.25), calls=%async_computation | async-start | bytes 131072 | tf_op jit(solution)/shard_map/all_to_all | solution.py:88
  103.3 41.4 %all-to-all-start.1 = ((bf16[128,8,128]{2,1,0:T(8,128)(2,1)}), bf16[128,8,128]{2,1,0:T(8,128)(2,1)S(1)}, u32[]{:S(2)}, u32[]{:S(2)}) async-start(bf16[128,8,128]{2,1,0:T(8,128)(2,1)} %scatter_fusion.1), calls=%async_computation.1 | async-start | bytes 524288 | tf_op jit(solution)/shard_map/all_to_all | solution.py:87
  119.4 85.6 %reduce-scatter.5.cloned.1.call-start = ((), (), s32[]{:S(2)}) async-start(), calls=%async_computation.5 | async-start | bytes 20480 | tf_op jit(solution)/shard_map/reduce_scatter | solution.py:105
  168.1 12.5 %copy-start.4 = (bf16[512,128]{1,0:T(8,128)(2,1)S(1)}, bf16[512,128]{1,0:T(8,128)(2,1)}, u32[]{:S(2)}) copy-start(bf16[512,128]{1,0:T(8,128)(2,1)} %param.20) | copy-start | bytes 393220
  168.1 36.9 %copy-start.6 = (f32[128]{0:T(128)S(1)}, f32[128]{0:T(128)}, u32[]{:S(2)}) copy-start(f32[128]{0:T(128)} %param.17) | copy-start | bytes 1540
  168.1 46.3 %copy-start.7 = (f32[128]{0:T(128)S(1)}, f32[128]{0:T(128)}, u32[]{:S(2)}) copy-start(f32[128]{0:T(128)} %param.19) | copy-start | bytes 1540
  168.1 46.3 %copy-start.8 = (f32[128]{0:T(128)S(1)}, f32[128]{0:T(128)}, u32[]{:S(2)}) copy-start(f32[128]{0:T(128)} %param.18) | copy-start | bytes 1540
  168.1 57.5 %copy-start.2 = (bf16[512,128]{1,0:T(8,128)(2,1)S(1)}, bf16[512,128]{1,0:T(8,128)(2,1)}, u32[]{:S(2)}) copy-start(bf16[512,128]{1,0:T(8,128)(2,1)} %param.22) | copy-start | bytes 393220
  168.1 57.6 %copy-start.3 = (bf16[512,128]{1,0:T(8,128)(2,1)S(1)}, bf16[512,128]{1,0:T(8,128)(2,1)}, u32[]{:S(2)}) copy-start(bf16[512,128]{1,0:T(8,128)(2,1)} %param.21) | copy-start | bytes 393220
  180.6 161.0 %reduce-scatter.7.cloned.1.call-start = ((), (), s32[]{:S(2)}) async-start(), calls=%async_computation.6 | async-start | bytes 655360
Sparse Core Ops, SparseCore 0:
  10.5 157.5 all-gather.1
  180.7 24.3 reduce-scatter.4
  314.7 26.7 reduce-scatter.6
where the time goes:
time: 351 us; the launch traced here: 350 us
  blocking collectives  117 us (33%)
  waiting for transfers between devices  81.5 us (23%)
  local copies, waits for them, and re-layouts  81.4 us (23%)
  starting transfers between devices  35.8 us (10%)
  matrix products  15.3 us (4%)
  between operations  13.4 us (4%)
  other arithmetic  5.44 us (2%)
    all_gather x1, blocking collectives, local(): every_key = lax.all_gather(key_value, 'seq', axis=0, tiled=True)  84.1 us
    scatter x1, local copies, waits for them, and re-layouts, local(): jnp.zeros((devices, capacity, quarter), jnp.bfloat16).at[owner, ranks]  51.3 us
    unnamed x4, waiting for transfers between devices  27.7 us
    reduce_scatter x1, waiting for transfers between devices, local(): lax.psum_scatter(partial_conv, 'head', scatter_dimension=1, tiled=True)  24.1 us
    scatter x1, local copies, waits for them, and re-layouts, local(): jnp.full((devices, capacity), -1, jnp.int32).at[owner, ranks].set(target)  22 us
    all_gather x1, waiting for transfers between devices, local(): lax.all_gather(conv_weight, 'seq', axis=0, tiled=True)  20 us
    all_to_all x1, starting transfers between devices, local(): lax.all_to_all(where_to, 'seq', split_axis=0, concat_axis=0, tiled=True)  19.5 us
    all_to_all x1, starting transfers between devices, local(): lax.all_to_all(outgoing, 'seq', split_axis=0, concat_axis=0, tiled=True)  16.2 us
  transfers between devices with their start and end apart: 5, of which 4 were waited for; matrix products, arithmetic and copies ran while one was open for 23% of the time, Pallas kernels for 0%

commit v1 on v0

--- a/solution.py
+++ b/solution.py
@@ -129,7 +129,9 @@
         jnp.zeros((local_rows, heads_here, HEAD_SIZE), jnp.float32),
     )
     folder = make_fold(queries, heads_here, scale)
-    every_key = lax.all_gather(key_value, "seq", axis=0, tiled=True)
+    every_key = jnp.concatenate(
+        lax.all_to_all(jnp.stack([key_value] * lax.axis_size("seq")), "seq", 0, 0), axis=0
+    )
     highest, totals, accum = folder(start_state, every_key, 0)
     attended = (accum / totals.T[:, :, None]).reshape(local_rows, quarter).astype(jnp.bfloat16)
     projected = jnp.dot(attended, out_weight, preferred_element_type=jnp.float32)

time: 351 us -> 311 us (0.89)
  blocking collectives: 117 us -> 33 us
  waiting for transfers between devices: 81.5 us -> 108 us
  starting transfers between devices: 35.8 us -> 52.4 us
    all_gather x1 -> x0, blocking collectives: 84.1 us -> none  [local(): every_key = lax.all_gather(key_value, 'seq', axis=0, tiled=True)]
    all_to_all x0 -> x1, waiting for transfers between devices: none -> 19.2 us  [local(): lax.all_to_all(jnp.stack([key_value] * lax.axis_size('seq')), 'seq', 0, 0)]
    all_to_all x0 -> x1, starting transfers between devices: none -> 16.6 us  [local(): lax.all_to_all(jnp.stack([key_value] * lax.axis_size('seq')), 'seq', 0, 0)]
    all_to_all x1, waiting for transfers between devices: 9.73 us -> 23.8 us  [local(): lax.all_to_all(outgoing, 'seq', split_axis=0, concat_axis=0, tiled=True)]
    unnamed x4, waiting for transfers between devices: 27.7 us -> 20.9 us
  transfers between devices with their start and end apart: 5 -> 6, of which waited for: 4 -> 5; matrix products, arithmetic and copies ran while one was open for 23% -> 26% of each run, Pallas kernels for 0% -> 0%
where the time goes in v1:
time: 311 us; the launch traced here: 310 us
  waiting for transfers between devices  108 us (35%)
  local copies, waits for them, and re-layouts  82.2 us (26%)
  starting transfers between devices  52.4 us (17%)
  blocking collectives  33 us (11%)
  matrix products  15.3 us (5%)
  between operations  13.4 us (4%)
  other arithmetic  5.44 us (2%)
    scatter x1, local copies, waits for them, and re-layouts, local(): jnp.zeros((devices, capacity, quarter), jnp.bfloat16).at[owner, ranks]  51.3 us
    reduce_scatter x1, waiting for transfers between devices, local(): lax.psum_scatter(partial_conv, 'head', scatter_dimension=1, tiled=True)  24.5 us
    all_to_all x1, waiting for transfers between devices, local(): lax.all_to_all(outgoing, 'seq', split_axis=0, concat_axis=0, tiled=True)  23.8 us
    scatter x1, local copies, waits for them, and re-layouts, local(): jnp.full((devices, capacity), -1, jnp.int32).at[owner, ranks].set(target)  22 us
    unnamed x4, waiting for transfers between devices  20.9 us
    all_gather x1, waiting for transfers between devices, local(): lax.all_gather(conv_weight, 'seq', axis=0, tiled=True)  20 us
    all_to_all x1, starting transfers between devices, local(): lax.all_to_all(where_to, 'seq', split_axis=0, concat_axis=0, tiled=True)  19.5 us
    all_to_all x1, waiting for transfers between devices, local(): lax.all_to_all(jnp.stack([key_value] * lax.axis_size('seq')), 'seq', 0, 0)  19.2 us
  transfers between devices with their start and end apart: 6, of which 5 were waited for; matrix products, arithmetic and copies ran while one was open for 26% of the time, Pallas kernels for 0%

profile of v1, /device:TPU:2, one launch (start us, length us, event | category | flops | bytes accessed | tf_op | source)
XLA Modules:
  0.0 310.1 jit_solution(6646319603645169918)
XLA Ops:
  6.5 0.7 all-gather.2.cloned.1.call-update
  7.3 0.7 fusion.28
  8.7 22.0 %scatter_fusion = s32[128,8]{0,1:T(8,128)S(1)} fusion(s32[128,8]{0,1:T(8,128)S(1)} %broadcast_in_dim.22, s32[512]{0:T(512)S(1)} %bitcast.79, s32[512]{0:T(512)S(1)} %get-tuple-element.91), kind=kCustom, calls=%fused_computation | custom fusion | bytes 10240 | tf_op jit(solution)/shard_map/scatter | solution.py:85
  30.7 0.7 copy.24
  31.5 19.5 %all-to-all-start = ((s32[128,1,8]{2,1,0:T(1,128)}), s32[128,1,8]{2,1,0:T(1,128)S(1)}, u32[]{:S(2)}, u32[]{:S(2)}) async-start(s32[128,1,8]{2,1,0:T(1,128)} %copy.24), calls=%async_computation | async-start | bytes 131072 | tf_op jit(solution)/shard_map/all_to_all | solution.py:88
  51.2 0.7 broadcast_in_dim.48
  51.9 51.3 %scatter_fusion.1 = bf16[128,8,128]{2,1,0:T(8,128)(2,1)} fusion(bf16[128,8,128]{2,1,0:T(8,128)(2,1)} %broadcast_in_dim.48, s32[512]{0:T(512)S(1)} %bitcast.80, bf16[512,128]{1,0:T(8,128)(2,1)S(1)} %broadcast_multiply_fusion), kind=kCustom, calls=%fused_computation.1 | custom fusion | bytes 397312 | tf_op jit(solution)/shard_map/scatter | solution.py:84
  103.3 16.2 %all-to-all-start.1 = ((bf16[128,8,128]{2,1,0:T(8,128)(2,1)}), bf16[128,8,128]{2,1,0:T(8,128)(2,1)S(1)}, u32[]{:S(2)}, u32[]{:S(2)}) async-start(bf16[128,8,128]{2,1,0:T(8,128)(2,1)} %scatter_fusion.1), calls=%async_computation.1 | async-start | bytes 524288 | tf_op jit(solution)/shard_map/all_to_all | solution.py:87
  119.5 0.5 broadcast.300
  120.0 0.8 reduce.3
  120.9 23.8 %all-to-all-done.1 = bf16[128,8,128]{2,1,0:T(8,128)(2,1)S(1)} async-done(((bf16[128,8,128]{2,1,0:T(8,128)(2,1)}), bf16[128,8,128]{2,1,0:T(8,128)(2,1)S(1)}, u32[]{:S(2)}, u32[]{:S(2)}) %all-to-all-start.1) | async-done | bytes 262176 | tf_op jit(solution)/shard_map/all_to_all | solution.py:87
  144.7 3.4 %scatter_custom_fusion.2 = bf16[513,128]{1,0:T(8,128)(2,1)S(1)} fusion(s32[1024]{0:T(1024)S(1)} %bitcast.94, bf16[128,8,128]{2,1,0:T(8,128)(2,1)S(1)} %all-to-all-done.1, bf16[]{:T(256)} %constant.103.clone.1), kind=kCustom, calls=%fused_computation.30 | custom fusion | bytes 393474 | tf_op jit(solution)/shard_map/scatter | solution.py:95
  148.1 20.0 %all-gather.2.cloned.1.call-done = bf16[512,64,128]{2,1,0:T(8,128)(2,1)} async-done(((bf16[4,64,128]{2,1,0:T(8,128)(2,1)}), bf16[512,64,128]{2,1,0:T(8,128)(2,1)}) %all-gather.2.cloned.1.call-update) | async-done | bytes 8388624 | tf_op jit(solution)/shard_map/all_gather | solution.py:101
  168.1 12.4 %fusion.13 = f32[8,512]{1,0:T(8,128)} fusion(bf16[512,64,128]{2,1,0:T(8,128)(2,1)} %all-gather.2.cloned.1.call-done, bf16[8,64,128]{2,1,0:T(8,128)(2,1)S(1)} %bitcast.87), kind=kOutput, calls=%fused_computation.25 | convolution fusion | flops 67108864 | bytes 8536064 | tf_op jit(solution)/shard_map/bpc,opc->bo/dot_general | solution.py:98
  180.5 24.5 %reduce-scatter.5.cloned.1.call-done = f32[8,128]{1,0:T(8,128)} async-done(((f32[8,512]{1,0:T(8,128)}), f32[8,128]{1,0:T(8,128)}) %reduce-scatter.5.cloned.1.call-update) | async-done | bytes 4112 | tf_op jit(solution)/shard_map/reduce_scatter | solution.py:105
  205.0 0.8 add_reduce_fusion
  205.8 8.6 %all-reduce = (f32[8]{0:T(128)S(1)}, f32[8]{0:T(128)S(1)}) all-reduce(f32[8]{0:T(128)S(1)} %get-tuple-element.74, f32[8]{0:T(128)S(1)} %get-tuple-element.73), channel_id=1, replica_groups=mesh['seq'=128,'head'=4] {'head'}, use_global_device_ids=true, to_apply=%region_10.11 | all-reduce | flops 16 | bytes 128 | tf_op jit(solution)/shard_map/psum | solution.py:107
  214.4 0.8 add_convert_fusion
  215.2 10.4 %all_gather.10 = bf16[8,512]{1,0:T(8,128)(2,1)S(1)} all-gather(bf16[8,128]{1,0:T(8,128)(2,1)S(1)} %add_convert_fusion), channel_id=1, replica_groups=mesh['seq'=128,'head'=4] {'head'}, dimensions={1}, use_global_device_ids=true | all-gather | bytes 10240 | tf_op jit(solution)/shard_map/all_gather | solution.py:113
  225.8 0.8 stack.2
  226.6 16.6 %all-to-all-start.2 = ((bf16[128,8,256]{2,1,0:T(8,128)(2,1)}), bf16[128,8,256]{2,1,0:T(8,128)(2,1)S(1)}, u32[]{:S(2)}, u32[]{:S(2)}) async-start(bf16[128,8,256]{2,1,0:T(8,128)(2,1)} %stack.2), calls=%async_computation.3 | async-start | bytes 1048576 | tf_op jit(solution)/shard_map/all_to_all | solution.py:133
  243.3 14.0 %all_gather.11 = bf16[512,512]{1,0:T(8,128)(2,1)S(1)} all-gather(bf16[512,128]{1,0:T(8,128)(2,1)S(1)} %copy-done.1), channel_id=1, replica_groups=mesh['seq'=128,'head'=4] {'head'}, dimensions={1}, use_global_device_ids=true | all-gather | bytes 655360 | tf_op jit(solution)/shard_map/all_gather | solution.py:119
  257.7 19.2 %all-to-all-done.2 = bf16[128,8,256]{2,1,0:T(8,128)(2,1)S(1)} async-done(((bf16[128,8,256]{2,1,0:T(8,128)(2,1)}), bf16[128,8,256]{2,1,0:T(8,128)(2,1)S(1)}, u32[]{:S(2)}, u32[]{:S(2)}) %all-to-all-start.2) | async-done | bytes 524320 | tf_op jit(solution)/shard_map/all_to_all | solution.py:133
  276.9 3.3 %while.15 = (s32[]{:T(128)}, f32[2,512]{1,0:T(2,128)S(1)}, f32[2,512]{1,0:T(2,128)S(1)}, f32[512,2,64]{0,2,1:T(8,128)S(1)}, bf16[2,512,256]{2,1,0:T(8,128)(2,1)S...) while((s32[]{:T(128)}, f32[2,512]{1,0:T(2,128)S(1)}, f32[2,512]{1,0:T(2,128)S(1)}, ...), condition=%wide.region_14.15_spmd.clone, body=%wide.region_11.14_spmd.clone.sunk | while | flops 138614784 | bytes 8847461 | solution.py:49
  277.1 0.5 bitcast_reduce_fusion.2
  277.6 0.5 fusion.67
  278.8 0.5 bitcast_reduce_fusion.2
  279.3 0.5 fusion.67
  280.6 1.0 copy.29
  281.6 20.1 %reduce-scatter.7.cloned.1.call-done = bf16[128,512]{1,0:T(8,128)(2,1)} async-done(((bf16[512,512]{1,0:T(8,128)(2,1)}), bf16[128,512]{1,0:T(8,128)(2,1)}) %reduce-scatter.7.cloned.1.call-update) | async-done | bytes 131088
  301.7 1.0 copy.30
  302.7 0.8 multiply_convert_fusion
  (64 shorter events, 3.2 us)
Async XLA Ops:
  6.5 273.7 %copy-start = (bf16[128,512]{1,0:T(8,128)(2,1)S(1)}, bf16[128,512]{1,0:T(8,128)(2,1)}, u32[]{:S(2)}) copy-start(bf16[128,512]{1,0:T(8,128)(2,1)} %param.23) | copy-start | bytes 393220
  6.5 161.6 %all-gather.2.cloned.1.call-start = ((), (), s32[]{:S(2)}) async-start(), calls=%async_computation.5 | async-start | bytes 8454144 | tf_op jit(solution)/shard_map/all_gather | solution.py:101
  8.7 42.3 %copy-start.5 = (s32[512]{0:T(512)S(1)}, s32[512]{0:T(512)}, u32[]{:S(2)}) copy-start(s32[512]{0:T(512)} %param.15) | copy-start | bytes 6148
  8.7 42.3 %copy-start.1 = (bf16[512,128]{1,0:T(8,128)(2,1)S(1)}, bf16[512,128]{1,0:T(8,128)(2,1)}, u32[]{:S(2)}) copy-start(bf16[512,128]{1,0:T(8,128)(2,1)} %param.13) | copy-start | bytes 393220
  31.5 71.8 %all-to-all-start = ((s32[128,1,8]{2,1,0:T(1,128)}), s32[128,1,8]{2,1,0:T(1,128)S(1)}, u32[]{:S(2)}, u32[]{:S(2)}) async-start(s32[128,1,8]{2,1,0:T(1,128)} %copy.24), calls=%async_computation | async-start | bytes 131072 | tf_op jit(solution)/shard_map/all_to_all | solution.py:88
  103.3 41.4 %all-to-all-start.1 = ((bf16[128,8,128]{2,1,0:T(8,128)(2,1)}), bf16[128,8,128]{2,1,0:T(8,128)(2,1)S(1)}, u32[]{:S(2)}, u32[]{:S(2)}) async-start(bf16[128,8,128]{2,1,0:T(8,128)(2,1)} %scatter_fusion.1), calls=%async_computation.1 | async-start | bytes 524288 | tf_op jit(solution)/shard_map/all_to_all | solution.py:87
  119.4 85.6 %reduce-scatter.5.cloned.1.call-start = ((), (), s32[]{:S(2)}) async-start(), calls=%async_computation.6 | async-start | bytes 20480 | tf_op jit(solution)/shard_map/reduce_scatter | solution.py:105
  168.1 36.9 %copy-start.6 = (f32[128]{0:T(128)S(1)}, f32[128]{0:T(128)}, u32[]{:S(2)}) copy-start(f32[128]{0:T(128)} %param.17) | copy-start | bytes 1540
  168.1 46.3 %copy-start.7 = (f32[128]{0:T(128)S(1)}, f32[128]{0:T(128)}, u32[]{:S(2)}) copy-start(f32[128]{0:T(128)} %param.19) | copy-start | bytes 1540
  168.1 46.3 %copy-start.8 = (f32[128]{0:T(128)S(1)}, f32[128]{0:T(128)}, u32[]{:S(2)}) copy-start(f32[128]{0:T(128)} %param.18) | copy-start | bytes 1540
  168.1 57.4 %copy-start.2 = (bf16[512,128]{1,0:T(8,128)(2,1)S(1)}, bf16[512,128]{1,0:T(8,128)(2,1)}, u32[]{:S(2)}) copy-start(bf16[512,128]{1,0:T(8,128)(2,1)} %param.22) | copy-start | bytes 393220
  168.1 57.6 %copy-start.3 = (bf16[512,128]{1,0:T(8,128)(2,1)S(1)}, bf16[512,128]{1,0:T(8,128)(2,1)}, u32[]{:S(2)}) copy-start(bf16[512,128]{1,0:T(8,128)(2,1)} %param.21) | copy-start | bytes 393220
  180.5 76.9 %copy-start.4 = (bf16[512,128]{1,0:T(8,128)(2,1)S(1)}, bf16[512,128]{1,0:T(8,128)(2,1)}, u32[]{:S(2)}) copy-start(bf16[512,128]{1,0:T(8,128)(2,1)} %param.20) | copy-start | bytes 393220
  226.6 50.2 %all-to-all-start.2 = ((bf16[128,8,256]{2,1,0:T(8,128)(2,1)}), bf16[128,8,256]{2,1,0:T(8,128)(2,1)S(1)}, u32[]{:S(2)}, u32[]{:S(2)}) async-start(bf16[128,8,256]{2,1,0:T(8,128)(2,1)} %stack.2), calls=%async_computation.3 | async-start | bytes 1048576 | tf_op jit(solution)/shard_map/all_to_all | solution.py:133
  243.3 58.5 %reduce-scatter.7.cloned.1.call-start = ((), (), s32[]{:S(2)}) async-start(), calls=%async_computation.7 | async-start | bytes 655360
Sparse Core Ops, SparseCore 0:
  10.5 157.5 all-gather.1
  180.6 24.3 reduce-scatter.4
  281.7 19.9 reduce-scatter.6
